TPU v7x, 128 devices: a whole 4x4x4 slice. The times are simulated.
128 devices in a mesh: dp: 16 (over x, z_lo, core), pipe: 8 (over y, z_hi).
Axes of the slice: x: 4, y: 4, z: 4 (z_hi: 2, z_lo: 2; z = z_hi * 2 + z_lo), core: 2. Of those that a mesh axis runs over, the one named last changes fastest.
Arguments:
- shallow: bfloat16 [4096, 8192], P('dp'), may hold values from -8 to 8
- teacher: bfloat16 [4096, 8192], P(('dp', 'pipe')), may hold values from -8 to 8
- positions: int32 [4096], P('dp'), may hold values from 0 to 4095
- segments: int32 [4096], P('dp'), may hold values from 0 to 255, never falling along the last dimension, each value on 1 to 64 neighbouring positions
- in_gain: float32 [8192], replicated, may hold values from 0.2 to 4.5
- w_query: bfloat16 [8192, 4096], P('dp', 'pipe'), may hold values from -0.0625 to 0.0625
- w_keyval: bfloat16 [8192, 1024], P('dp', 'pipe'), may hold values from -0.0625 to 0.0625
- w_output: bfloat16 [4096, 8192], P('pipe', 'dp'), may hold values from -0.09375 to 0.09375
Outputs:
- loss: float32 [], replicated
- step_query: float32 [8192, 4096], P('dp', 'pipe')
- step_keyval: float32 [8192, 1024], P('dp', 'pipe')
- step_output: float32 [4096, 8192], P('pipe', 'dp')
Inputs may be any that keep to these rules, and one draw needn't show every extreme that they name: `segments`: ids never fall along the rows; every segment covers 1 to 64 rows.
All inputs are finite; a program needn't handle non-finite values.
Results may differ from a plain program's by a relative error of at most 0.023.
Values may be sent and summed in bfloat16 or wider, within the bound.
A program may use at most 128 MiB of HBM per device.

v0:
```python
import math
import jax
import jax.numpy as jnp
from jax import lax
from jax.sharding import PartitionSpec as P

D = 8192
HD = 128
QH = 32
KV = 4
theta_base = 10000.0
norm_eps = 1e-05
cosine_eps = 1e-06
mean_eps = 1e-12
mask_fill = -1e30


def shifted(value, axis, steps):
    count = lax.axis_size(axis)
    pairs = [(source, (source + steps) % count) for source in range(count)]
    return lax.ppermute(value, axis, pairs)


def normalize_rows(rows_in, in_gain):
    widened = rows_in.astype(jnp.float32)
    spread = jnp.mean(widened * widened, axis=-1, keepdims=True)
    return (widened * lax.rsqrt(spread + norm_eps) * in_gain[None, :]).astype(jnp.bfloat16)


def rotary_tables(positions, head_width):
    half_width = head_width // 2
    exponent = jnp.arange(half_width).astype(jnp.float32) * (2.0 / head_width)
    inverse = jnp.power(jnp.float32(theta_base), -exponent)
    angle_table = positions.astype(jnp.float32)[:, None] * inverse[None, :]
    return (jnp.cos(angle_table), jnp.sin(angle_table))


def rotate(values, cosine, sine_table):
    half_width = values.shape[-1] // 2
    leading = values[..., :half_width]
    trailing = values[..., half_width:]
    cosine_row = cosine[:, None, :]
    sine_row = sine_table[:, None, :]
    return jnp.concatenate(
        [leading * cosine_row - trailing * sine_row, trailing * cosine_row + leading * sine_row],
        axis=-1,
    )


def unrotate(values, cosine, sine_table):
    half_width = values.shape[-1] // 2
    leading = values[..., :half_width]
    trailing = values[..., half_width:]
    cosine_row = cosine[:, None, :]
    sine_row = sine_table[:, None, :]
    return jnp.concatenate(
        [leading * cosine_row + trailing * sine_row, trailing * cosine_row - leading * sine_row],
        axis=-1,
    )


def attend(queries, keys_head, values_head, allowed):
    score_scale = 1.0 / math.sqrt(queries.shape[-1])
    scores = (
        jnp.einsum("rhd,khd->hrk", queries, keys_head, preferred_element_type=jnp.float32)
        * score_scale
    )
    scores = jnp.where(allowed[None], scores, mask_fill)
    highest = jnp.max(scores, axis=-1, keepdims=True)
    weights = jnp.exp(scores - highest)
    softmax_rows = weights / jnp.sum(weights, axis=-1, keepdims=True)
    softmax_low = softmax_rows.astype(jnp.bfloat16)
    attended = jnp.einsum(
        "hrk,khd->rhd", softmax_low, values_head, preferred_element_type=jnp.float32
    ).astype(jnp.bfloat16)
    return (softmax_rows, softmax_low, attended)


def attend_grad(softmax_rows, softmax_low, queries, keys_head, values_head, att_grad):
    score_scale = 1.0 / math.sqrt(queries.shape[-1])
    inner_prod = jnp.einsum(
        "rhd,khd->hrk", att_grad, values_head, preferred_element_type=jnp.float32
    )
    centred = inner_prod - jnp.sum(softmax_rows * inner_prod, axis=-1, keepdims=True)
    score_grad = (softmax_rows * centred * score_scale).astype(jnp.bfloat16)
    query_part = jnp.einsum(
        "hrk,khd->rhd", score_grad, keys_head, preferred_element_type=jnp.float32
    )
    key_part = jnp.einsum("hrk,rhd->khd", score_grad, queries, preferred_element_type=jnp.float32)
    value_part = jnp.einsum(
        "hrk,rhd->khd", softmax_low, att_grad, preferred_element_type=jnp.float32
    )
    return (query_part, key_part, value_part)


def held_low(values):
    return lax.optimization_barrier(values.astype(jnp.bfloat16)).astype(jnp.float32)


def contract_rows(left, right):
    return lax.dot_general(
        left, right, (((0,), (0,)), ((), ())), preferred_element_type=jnp.float32
    )


def contract_cols(left, right):
    return lax.dot_general(
        left, right, (((1,), (1,)), ((), ())), preferred_element_type=jnp.float32
    )


def per_device(shallow, teacher, positions, segments, in_gain, w_query, w_keyval, w_output):
    group_rows = shallow.shape[0]
    pipe_count = lax.axis_size("pipe")
    data_count = lax.axis_size("dp")
    pipe_rank = lax.axis_index("pipe")
    block_rows = group_rows // pipe_count
    head_cols = w_query.shape[1]
    local_heads = head_cols // HD
    keyval_cols = w_keyval.shape[1]
    keyval_blocks = keyval_cols // HD
    all_rows = group_rows * data_count
    param_count = D * (2 * QH * HD + 2 * KV * HD)
    normed = normalize_rows(shallow, in_gain)
    cosine, sine_table = rotary_tables(positions, HD)
    columns = normed
    query_proj = jnp.dot(
        columns,
        lax.all_gather(w_query, "dp", axis=0, tiled=True),
        preferred_element_type=jnp.float32,
    )
    keyval_proj = jnp.dot(
        columns,
        lax.all_gather(w_keyval, "dp", axis=0, tiled=True),
        preferred_element_type=jnp.float32,
    )
    queries = rotate(query_proj.reshape(group_rows, local_heads, HD), cosine, sine_table).astype(
        jnp.bfloat16
    )
    keyval_local = keyval_proj.reshape(group_rows, keyval_blocks, HD)
    block_ids = pipe_rank * keyval_blocks + jnp.arange(keyval_blocks)
    is_key = (block_ids % 2 == 0)[None, :, None]
    keyval_local = jnp.where(is_key, rotate(keyval_local, cosine, sine_table), keyval_local).astype(
        jnp.bfloat16
    )
    keyval_all = lax.all_gather(
        keyval_local.reshape(group_rows, keyval_cols), "pipe", axis=1, tiled=True
    )
    keyval_all = keyval_all.reshape(group_rows, KV, 2, HD)
    head_ids = pipe_rank * local_heads + jnp.arange(local_heads)
    chooser = head_ids[:, None] % KV == jnp.arange(KV)[None, :]
    picked = jnp.einsum(
        "rksd,jk->rjsd",
        keyval_all,
        chooser.astype(jnp.bfloat16),
        preferred_element_type=jnp.float32,
    ).astype(jnp.bfloat16)
    keys_head = picked[:, :, 0]
    values_head = picked[:, :, 1]
    row_order = jnp.arange(group_rows)
    allowed = (segments[:, None] == segments[None, :]) & (row_order[None, :] <= row_order[:, None])
    softmax_rows, softmax_low, attended = attend(queries, keys_head, values_head, allowed)
    att_flat = attended.reshape(group_rows, head_cols)
    shallow_block = lax.dynamic_slice_in_dim(shallow, pipe_rank * block_rows, block_rows, 0)
    target = shifted(teacher, "pipe", 1).astype(jnp.float32)
    w_out_full = lax.all_gather(w_output, "dp", axis=1, tiled=True)
    partial_value = held_low(jnp.dot(att_flat, w_out_full, preferred_element_type=jnp.float32))
    out_rows = lax.psum_scatter(
        partial_value.astype(jnp.bfloat16), "pipe", scatter_dimension=0, tiled=True
    ).astype(jnp.float32)
    output = shallow_block.astype(jnp.float32) + out_rows
    norm_out = jnp.sqrt(jnp.sum(output * output, axis=-1, keepdims=True) + cosine_eps)
    norm_tar = jnp.sqrt(jnp.sum(target * target, axis=-1, keepdims=True) + cosine_eps)
    cosine_sim = jnp.sum(output * target, axis=-1, keepdims=True) / (norm_out * norm_tar)
    loss_local = jnp.sum(1.0 - cosine_sim)
    out_grad = (
        -(target / (norm_out * norm_tar) - cosine_sim * output / (norm_out * norm_out)) / all_rows
    ).astype(jnp.bfloat16)
    loss_total = lax.psum(loss_local, ("dp", "pipe"))
    grad_all = lax.all_gather(out_grad, "pipe", axis=0, tiled=True)
    att_grad = contract_cols(grad_all, w_out_full).astype(jnp.bfloat16)
    att_grad = att_grad.reshape(group_rows, local_heads, HD)
    query_part, key_part, value_part = attend_grad(
        softmax_rows, softmax_low, queries, keys_head, values_head, att_grad
    )
    query_grad = (
        unrotate(query_part, cosine, sine_table).astype(jnp.bfloat16).reshape(group_rows, head_cols)
    )
    spread_back = jnp.einsum(
        "rjsd,jk->rksd", jnp.stack([key_part, value_part], axis=2), chooser.astype(jnp.float32)
    )
    keyval_sum = lax.psum_scatter(
        spread_back.reshape(group_rows, 2 * KV * HD).astype(jnp.bfloat16),
        "pipe",
        scatter_dimension=1,
        tiled=True,
    ).astype(jnp.float32)
    keyval_sum = keyval_sum.reshape(group_rows, keyval_blocks, HD)
    keyval_grad = (
        jnp.where(is_key, unrotate(keyval_sum, cosine, sine_table), keyval_sum)
        .astype(jnp.bfloat16)
        .reshape(group_rows, keyval_cols)
    )
    grad_inputs = jnp.concatenate([query_grad, keyval_grad], axis=1)
    columns = normed
    grad_shard = lax.psum_scatter(
        jnp.concatenate(
            [contract_rows(columns, grad_inputs), contract_rows(grad_all, att_flat)], axis=1
        ).astype(jnp.bfloat16),
        "dp",
        scatter_dimension=0,
        tiled=True,
    ).astype(jnp.float32)
    grad_query = grad_shard[:, :head_cols]
    grad_keyval = grad_shard[:, head_cols : head_cols + keyval_cols]
    grad_output = grad_shard[:, head_cols + keyval_cols :].T
    squares = (
        jnp.sum(grad_query * grad_query)
        + jnp.sum(grad_keyval * grad_keyval)
        + jnp.sum(grad_output * grad_output)
    )
    square_total = lax.psum(squares, ("dp", "pipe"))
    grad_rms = jnp.sqrt(square_total / param_count + mean_eps)
    return (
        loss_total / all_rows,
        grad_query / grad_rms,
        grad_keyval / grad_rms,
        grad_output / grad_rms,
    )


def solution(mesh):
    placed = (
        P("dp", None),
        P(("dp", "pipe"), None),
        P("dp"),
        P("dp"),
        P(),
        P("dp", "pipe"),
        P("dp", "pipe"),
        P("pipe", "dp"),
    )
    return jax.shard_map(
        per_device,
        mesh=mesh,
        in_specs=placed,
        out_specs=(P(), P("dp", "pipe"), P("dp", "pipe"), P("pipe", "dp")),
        check_vma=False,
    )
```

profile of v0, /device:TPU:1, one launch (start us, length us, event | category | flops | bytes accessed | tf_op | source)
XLA Modules:
  0.0 725.1 jit_solution(165572289338817264)
XLA Ops:
  10.2 3.1 fusion.2
  13.3 0.9 fusion.32
  14.7 32.7 %all-gather.5.cloned.1.call-done = bf16[8192,128]{1,0:T(8,128)(2,1)} async-done(((bf16[512,128]{1,0:T(8,128)(2,1)}), bf16[8192,128]{1,0:T(8,128)(2,1)}) %all-gather.5.cloned.1.call-update) | async-done | bytes 2097168 | tf_op jit(solution)/shard_map/all_gather | solution.py:134
  47.4 4.6 fusion.72
  52.4 29.5 %all_gather.16 = bf16[256,1024]{0,1:T(8,128)(2,1)S(1)} all-gather(bf16[256,128]{0,1:T(8,128)(2,1)S(1)} %fusion.37), channel_id=1, replica_groups=mesh['dp'=16,'pipe'=8] {'pipe'}, dimensions={1}, use_global_device_ids=true | all-gather | bytes 589824 | tf_op jit(solution)/shard_map/all_gather | solution.py:146
  83.0 26.8 %all-gather.7.cloned.1.call-done = bf16[8192,512]{1,0:T(8,128)(2,1)} async-done(((bf16[512,512]{1,0:T(8,128)(2,1)}), bf16[8192,512]{1,0:T(8,128)(2,1)}) %all-gather.7.cloned.1.call-update) | async-done | bytes 8388624 | tf_op jit(solution)/shard_map/all_gather | solution.py:129
  109.8 7.0 fusion.70
  118.4 45.1 %all-gather.9.cloned.1.call-done = bf16[512,8192]{1,0:T(8,128)(2,1)} async-done(((bf16[512,512]{1,0:T(8,128)(2,1)}), bf16[512,8192]{1,0:T(8,128)(2,1)}) %all-gather.9.cloned.1.call-update) | async-done | bytes 8388624 | tf_op jit(solution)/shard_map/all_gather | solution.py:166
  163.5 7.8 %convolution_convert_fusion.2 = bf16[256,8192]{1,0:T(8,128)(2,1)} fusion(bf16[256,512]{0,1:T(8,128)(2,1)S(1)} %bitcast.64, bf16[512,8192]{1,0:T(8,128)(2,1)} %all-gather.9.cloned.1.call-done), kind=kOutput, calls=%fused_computation.7 | convolution fusion | flops 2149580800 | bytes 12845056 | tf_op jit(solution)/shard_map/dot_general | solution.py:167
  171.4 2.9 collective-permute-start
  174.3 15.5 %collective-permute-done = bf16[32,8192]{1,0:T(8,128)(2,1)S(1)} collective-permute-done((bf16[32,8192]{1,0:T(8,128)(2,1)S(1)}, bf16[32,8192]{1,0:T(8,128)(2,1)S(1)}, u32[]{:S(2)}, u32[]{:S(2)}) %collective-permute-start) | collective-permute-done | bytes 524320 | tf_op jit(solution)/shard_map/ppermute | solution.py:21
  189.8 69.8 %reduce-scatter.4.cloned.1.call-done = bf16[32,8192]{1,0:T(8,128)(2,1)} async-done(((bf16[256,8192]{1,0:T(8,128)(2,1)}), bf16[32,8192]{1,0:T(8,128)(2,1)}) %reduce-scatter.4.cloned.1.call-update) | async-done | bytes 524304 | tf_op jit(solution)/shard_map/reduce_scatter | solution.py:168
  259.6 1.7 multiply_reduce_fusion.2
  261.9 2.4 fusion.19
  264.4 71.0 %all-gather.11.cloned.1.call-done = bf16[256,8192]{1,0:T(8,128)(2,1)} async-done(((bf16[32,8192]{1,0:T(8,128)(2,1)}), bf16[256,8192]{1,0:T(8,128)(2,1)}) %all-gather.11.cloned.1.call-update) | async-done | bytes 4194320 | tf_op jit(solution)/shard_map/all_gather | solution.py:180
  335.3 7.0 convolution_convert_fusion.6
  343.1 2.1 convolution_bitcast_fusion.1
  345.3 2.1 convolution_bitcast_fusion.2
  348.2 1.1 copy.51
  349.9 7.9 %convolution_convert_fusion.1 = bf16[8192,512]{0,1:T(8,128)(2,1)} fusion(bf16[256,512]{0,1:T(8,128)(2,1)S(1)} %bitcast.65, bf16[256,8192]{1,0:T(8,128)(2,1)} %all-gather.11.cloned.1.call-done), kind=kOutput, calls=%fused_computation.4 | convolution fusion | flops 2151677952 | bytes 12845056 | tf_op jit(solution)/shard_map/dot_general | solution.py:101
  357.8 58.6 %reduce-scatter.6.cloned.1.call-done = bf16[256,128]{0,1:T(8,128)(2,1)} async-done(((bf16[256,1024]{0,1:T(8,128)(2,1)}), bf16[256,128]{0,1:T(8,128)(2,1)}) %reduce-scatter.6.cloned.1.call-update) | async-done | bytes 65552 | tf_op jit(solution)/shard_map/reduce_scatter | solution.py:192
  416.5 0.8 convert_bitcast_fusion
  417.6 0.9 fusion.36
  418.5 5.8 convolution_convert_fusion
  424.3 13.8 %pad_maximum_fusion = bf16[8192,1152]{0,1:T(8,128)(2,1)} fusion(bf16[8192,512]{0,1:T(8,128)(2,1)} %convolution_convert_fusion.1, bf16[8192,640]{0,1:T(8,128)(2,1)S(1)} %convolution_convert_fusion), kind=kLoop, calls=%fused_computation.2 | loop fusion | flops 37748736 | bytes 37748736 | tf_op jit(solution)/shard_map/concatenate | solution.py:207
  438.1 203.0 %reduce-scatter.8.cloned.1.call-done = bf16[512,1152]{0,1:T(8,128)(2,1)} async-done(((bf16[8192,1152]{0,1:T(8,128)(2,1)}), bf16[512,1152]{0,1:T(8,128)(2,1)}) %reduce-scatter.8.cloned.1.call-update) | async-done | bytes 1179664 | tf_op jit(solution)/shard_map/reduce_scatter | solution.py:206
  641.1 1.6 convert_element_type.111
  643.4 0.9 multiply_reduce_fusion
  646.2 64.6 %all-reduce = (f32[]{:T(128)}, f32[]{:T(128)}) all-reduce(f32[]{:T(128)} %get-tuple-element.19, f32[]{:T(128)S(6)} %add.123), channel_id=1, replica_groups=mesh['dp'=16,'pipe'=8] {'dp','pipe'}, use_global_device_ids=true, to_apply=%region_8.9 | all-reduce | flops 2 | bytes 16 | tf_op jit(solution)/shard_map/psum | solution.py:179
  712.2 1.2 divide_bitcast_fusion
  713.4 1.8 copy.53
  715.2 1.3 copy.52
  (51 shorter events, 11.2 us)
Async XLA Ops:
  7.2 40.2 %all-gather.5.cloned.1.call-start = ((), (), s32[]{:S(2)}) async-start(), calls=%async_computation.3 | async-start | bytes 2228224 | tf_op jit(solution)/shard_map/all_gather | solution.py:134
  7.9 101.9 %all-gather.7.cloned.1.call-start = ((), (), s32[]{:S(2)}) async-start(), calls=%async_computation.4 | async-start | bytes 8912896 | tf_op jit(solution)/shard_map/all_gather | solution.py:129
  8.6 154.9 %all-gather.9.cloned.1.call-start = ((), (), s32[]{:S(2)}) async-start(), calls=%async_computation.5 | async-start | bytes 8912896 | tf_op jit(solution)/shard_map/all_gather | solution.py:166
  9.4 250.3 %reduce-scatter.4.cloned.1.call-start = ((), (), s32[]{:S(2)}) async-start(), calls=%async_computation.6 | async-start | bytes 4718592 | tf_op jit(solution)/shard_map/reduce_scatter | solution.py:168
  10.1 99.7 %copy-start = (f32[8192]{0:T(1024)S(1)}, f32[8192]{0:T(1024)}, u32[]{:S(2)}) copy-start(f32[8192]{0:T(1024)} %param.12) | copy-start | bytes 98308
  118.1 45.4 %copy-start.2 = (f32[4,256,256]{1,2,0:T(8,128)}, f32[4,256,256]{1,2,0:T(8,128)S(1)}, u32[]{:S(2)}) copy-start(f32[4,256,256]{1,2,0:T(8,128)S(1)} %get-tuple-element.40) | copy-start | bytes 3145732
  163.5 7.9 %copy-start.1 = (bf16[32,8192]{1,0:T(8,128)(2,1)S(1)}, bf16[32,8192]{1,0:T(8,128)(2,1)}, u32[]{:S(2)}) copy-start(bf16[32,8192]{1,0:T(8,128)(2,1)} %param.9) | copy-start | bytes 1572868
  171.3 164.0 %all-gather.11.cloned.1.call-start = ((), (), s32[]{:S(2)}) async-start(), calls=%async_computation.7 | async-start | bytes 4718592 | tf_op jit(solution)/shard_map/all_gather | solution.py:180
  171.4 18.4 %collective-permute-start = (bf16[32,8192]{1,0:T(8,128)(2,1)S(1)}, bf16[32,8192]{1,0:T(8,128)(2,1)S(1)}, u32[]{:S(2)}, u32[]{:S(2)}) collective-permute-start(bf16[32,8192]{1,0:T(8,128)(2,1)S(1)} %copy-done.1), channel_id=1, source_target_pairs={{0,1},{1,2},{2,3},{3,4},{4,5},{5,6},{6,7},{7,0},{8,9},{9,10},{10,1... | collective-permute-start | bytes 1572872 | tf_op jit(solution)/shard_map/ppermute | solution.py:21
  264.3 78.2 %copy-start.3 = (f32[4,256,256]{1,2,0:T(8,128)S(1)}, f32[4,256,256]{1,2,0:T(8,128)}, u32[]{:S(2)}) copy-start(f32[4,256,256]{1,2,0:T(8,128)} %copy-done.2) | copy-start | bytes 3145732
  264.3 152.1 %reduce-scatter.6.cloned.1.call-start = ((), (), s32[]{:S(2)}) async-start(), calls=%async_computation.8 | async-start | bytes 589824 | tf_op jit(solution)/shard_map/reduce_scatter | solution.py:192
  349.3 291.8 %reduce-scatter.8.cloned.1.call-start = ((), (), s32[]{:S(2)}) async-start(), calls=%async_computation.9 | async-start | bytes 20054016 | tf_op jit(solution)/shard_map/reduce_scatter | solution.py:206
Sparse Core Ops, SparseCore 0:
  9.7 37.6 all-gather.4
  49.1 60.6 all-gather.6
  111.5 51.9 all-gather.8
  171.4 88.1 reduce-scatter.3
  264.4 70.8 all-gather.10
  349.4 66.9 reduce-scatter.5
  438.2 202.8 reduce-scatter.7
where the time goes:
time: 726 us; the launch traced here: 725 us
  waiting for transfers between devices  525 us (72%)
  blocking collectives  94 us (13%)
  matrix products  46.8 us (6%)
  other arithmetic  31.7 us (4%)
  between operations  18.8 us (3%)
    reduce_scatter x1, waiting for transfers between devices, per_device(): lax.psum_scatter(jnp.concatenate([contract_rows(columns, grad_inputs), co...  203 us
    all_gather x1, waiting for transfers between devices, per_device(): grad_all = lax.all_gather(out_grad, 'pipe', axis=0, tiled=True)  71 us
    reduce_scatter x1, waiting for transfers between devices, per_device(): lax.psum_scatter(partial_value.astype(jnp.bfloat16), 'pipe', scatter_dime...  69.8 us
    psum x1, blocking collectives, per_device(): loss_total = lax.psum(loss_local, ('dp', 'pipe'))  64.6 us
    reduce_scatter x1, waiting for transfers between devices, per_device(): lax.psum_scatter(spread_back.reshape(group_rows, 2 * KV * HD).astype(jnp....  58.6 us
    all_gather x1, waiting for transfers between devices, per_device(): w_out_full = lax.all_gather(w_output, 'dp', axis=1, tiled=True)  45.1 us
    all_gather x1, waiting for transfers between devices, per_device(): lax.all_gather(w_keyval, 'dp', axis=0, tiled=True)  32.7 us
    all_gather x1, blocking collectives, per_device(): lax.all_gather(keyval_local.reshape(group_rows, keyval_cols), 'pipe', axi...  29.5 us
  transfers between devices with their start and end apart: 8, of which 8 were waited for; matrix products, arithmetic and copies ran while one was open for 4% of the time, Pallas kernels for 0%

commit v1 on v0

--- a/solution.py
+++ b/solution.py
@@ -13,6 +13,14 @@
 cosine_eps = 1e-06
 mean_eps = 1e-12
 mask_fill = -1e30
+
+
+def shapes_settle(u):
+    steps_seen = []
+    for _ in range(lax.axis_size("pipe")):
+        steps_seen.append(u)
+    carry_in = jnp.concatenate(lax.all_to_all(jnp.stack(steps_seen, axis=0), "pipe", 0, 0), axis=0)
+    return carry_in
 
 
 def shifted(value, axis, steps):
@@ -177,7 +185,7 @@
         -(target / (norm_out * norm_tar) - cosine_sim * output / (norm_out * norm_out)) / all_rows
     ).astype(jnp.bfloat16)
     loss_total = lax.psum(loss_local, ("dp", "pipe"))
-    grad_all = lax.all_gather(out_grad, "pipe", axis=0, tiled=True)
+    grad_all = shapes_settle(out_grad)
     att_grad = contract_cols(grad_all, w_out_full).astype(jnp.bfloat16)
     att_grad = att_grad.reshape(group_rows, local_heads, HD)
     query_part, key_part, value_part = attend_grad(

time: 726 us -> 708 us (0.975)
  waiting for transfers between devices: 525 us -> 457 us
  blocking collectives: 94 us -> 144 us
    all_gather x1 -> x0, waiting for transfers between devices: 71 us -> none  [per_device(): grad_all = lax.all_gather(out_grad, 'pipe', axis=0, tiled=True)]
    all_to_all x0 -> x1, blocking collectives: none -> 49.8 us  [shapes_settle(): lax.all_to_all(jnp.stack(steps_seen, axis=0), 'pipe', 0, 0)]
  transfers between devices with their start and end apart: 8 -> 7, of which waited for: 8 -> 7; matrix products, arithmetic and copies ran while one was open for 4% -> 4% of each run, Pallas kernels for 0% -> 0%
where the time goes in v1:
time: 708 us
  waiting for transfers between devices  457 us (65%)
  blocking collectives  144 us (20%)
  matrix products  45.5 us (6%)
  other arithmetic  30.9 us (4%)
  between operations  18.8 us (3%)
  local copies, waits for them, and re-layouts  8.46 us (1%)
    reduce_scatter x1, waiting for transfers between devices, per_device(): lax.psum_scatter(jnp.concatenate([contract_rows(columns, grad_inputs), co...  203 us
    reduce_scatter x1, waiting for transfers between devices, per_device(): lax.psum_scatter(partial_value.astype(jnp.bfloat16), 'pipe', scatter_dime...  69.8 us
    psum x1, blocking collectives, per_device(): loss_total = lax.psum(loss_local, ('dp', 'pipe'))  64.7 us
    reduce_scatter x1, waiting for transfers between devices, per_device(): lax.psum_scatter(spread_back.reshape(group_rows, 2 * KV * HD).astype(jnp....  61.6 us
    all_to_all x1, blocking collectives, shapes_settle(): lax.all_to_all(jnp.stack(steps_seen, axis=0), 'pipe', 0, 0)  49.8 us
    all_gather x1, waiting for transfers between devices, per_device(): w_out_full = lax.all_gather(w_output, 'dp', axis=1, tiled=True)  45.1 us
    all_gather x1, waiting for transfers between devices, per_device(): lax.all_gather(w_keyval, 'dp', axis=0, tiled=True)  32.7 us
    all_gather x1, blocking collectives, per_device(): lax.all_gather(keyval_local.reshape(group_rows, keyval_cols), 'pipe', axi...  29.5 us
  transfers between devices with their start and end apart: 7, of which 7 were waited for; matrix products, arithmetic and copies ran while one was open for 4% of the time, Pallas kernels for 0%

profile of v1, /device:TPU:1, one launch (start us, length us, event | category | flops | bytes accessed | tf_op | source)
XLA Modules:
  0.0 707.6 jit_solution(3399696065044364978)
XLA Ops:
  10.2 3.1 fusion.2
  13.3 0.9 fusion.32
  14.7 32.7 %all-gather.4.cloned.1.call-done = bf16[8192,128]{1,0:T(8,128)(2,1)} async-done(((bf16[512,128]{1,0:T(8,128)(2,1)}), bf16[8192,128]{1,0:T(8,128)(2,1)}) %all-gather.4.cloned.1.call-update) | async-done | bytes 2097168 | tf_op jit(solution)/shard_map/all_gather | solution.py:142
  47.4 4.6 fusion.72
  52.4 29.5 %all_gather.13 = bf16[256,1024]{0,1:T(8,128)(2,1)S(1)} all-gather(bf16[256,128]{0,1:T(8,128)(2,1)S(1)} %fusion.37), channel_id=1, replica_groups=mesh['dp'=16,'pipe'=8] {'pipe'}, dimensions={1}, use_global_device_ids=true | all-gather | bytes 589824 | tf_op jit(solution)/shard_map/all_gather | solution.py:154
  83.0 26.8 %all-gather.6.cloned.1.call-done = bf16[8192,512]{1,0:T(8,128)(2,1)} async-done(((bf16[512,512]{1,0:T(8,128)(2,1)}), bf16[8192,512]{1,0:T(8,128)(2,1)}) %all-gather.6.cloned.1.call-update) | async-done | bytes 8388624 | tf_op jit(solution)/shard_map/all_gather | solution.py:137
  109.8 7.0 fusion.70
  118.4 45.1 %all-gather.8.cloned.1.call-done = bf16[512,8192]{1,0:T(8,128)(2,1)} async-done(((bf16[512,512]{1,0:T(8,128)(2,1)}), bf16[512,8192]{1,0:T(8,128)(2,1)}) %all-gather.8.cloned.1.call-update) | async-done | bytes 8388624 | tf_op jit(solution)/shard_map/all_gather | solution.py:174
  163.5 7.8 %convolution_convert_fusion.2 = bf16[256,8192]{1,0:T(8,128)(2,1)} fusion(bf16[256,512]{0,1:T(8,128)(2,1)S(1)} %bitcast.67, bf16[512,8192]{1,0:T(8,128)(2,1)} %all-gather.8.cloned.1.call-done), kind=kOutput, calls=%fused_computation.7 | convolution fusion | flops 2149580800 | bytes 12845056 | tf_op jit(solution)/shard_map/dot_general | solution.py:175
  171.4 2.9 collective-permute-start
  174.3 15.5 %collective-permute-done = bf16[32,8192]{1,0:T(8,128)(2,1)S(1)} collective-permute-done((bf16[32,8192]{1,0:T(8,128)(2,1)S(1)}, bf16[32,8192]{1,0:T(8,128)(2,1)S(1)}, u32[]{:S(2)}, u32[]{:S(2)}) %collective-permute-start) | collective-permute-done | bytes 524320 | tf_op jit(solution)/shard_map/ppermute | solution.py:29
  189.8 69.8 %reduce-scatter.4.cloned.1.call-done = bf16[32,8192]{1,0:T(8,128)(2,1)} async-done(((bf16[256,8192]{1,0:T(8,128)(2,1)}), bf16[32,8192]{1,0:T(8,128)(2,1)}) %reduce-scatter.4.cloned.1.call-update) | async-done | bytes 524304 | tf_op jit(solution)/shard_map/reduce_scatter | solution.py:176
  259.6 1.7 multiply_reduce_fusion.2
  261.9 1.6 fusion.19
  264.0 49.8 %all_to_all.5 = bf16[8,32,8192]{2,1,0:T(8,128)(2,1)S(1)} all-to-all(bf16[8,32,8192]{2,1,0:T(8,128)(2,1)S(1)} %stack.8), channel_id=1, replica_groups=mesh['dp'=16,'pipe'=8] {'pipe'}, dimensions={0} | all-to-all | bytes 8388608 | tf_op jit(solution)/shard_map/all_to_all | solution.py:22
  313.8 2.0 copy-done
  315.7 5.7 convolution_convert_fusion.6
  322.2 2.1 convolution_bitcast_fusion.1
  324.4 2.1 convolution_bitcast_fusion.2
  327.3 1.1 copy.51
  329.3 7.9 %convolution_convert_fusion.1 = bf16[8192,512]{0,1:T(8,128)(2,1)} fusion(bf16[256,512]{0,1:T(8,128)(2,1)S(1)} %bitcast.68, bf16[256,8192]{1,0:T(8,128)(2,1)} %bitcast.63), kind=kOutput, calls=%fused_computation.4 | convolution fusion | flops 2151677952 | bytes 12845056 | tf_op jit(solution)/shard_map/dot_general | solution.py:109
  337.2 61.6 %reduce-scatter.6.cloned.1.call-done = bf16[256,128]{0,1:T(8,128)(2,1)} async-done(((bf16[256,1024]{0,1:T(8,128)(2,1)}), bf16[256,128]{0,1:T(8,128)(2,1)}) %reduce-scatter.6.cloned.1.call-update) | async-done | bytes 65552 | tf_op jit(solution)/shard_map/reduce_scatter | solution.py:200
  400.0 0.9 fusion.36
  400.8 5.8 convolution_convert_fusion
  406.6 13.8 %pad_maximum_fusion = bf16[8192,1152]{0,1:T(8,128)(2,1)} fusion(bf16[8192,512]{0,1:T(8,128)(2,1)} %convolution_convert_fusion.1, bf16[8192,640]{0,1:T(8,128)(2,1)S(1)} %convolution_convert_fusion), kind=kLoop, calls=%fused_computation.2 | loop fusion | flops 37748736 | bytes 37748736 | tf_op jit(solution)/shard_map/concatenate | solution.py:215
  420.5 203.0 %reduce-scatter.8.cloned.1.call-done = bf16[512,1152]{0,1:T(8,128)(2,1)} async-done(((bf16[8192,1152]{0,1:T(8,128)(2,1)}), bf16[512,1152]{0,1:T(8,128)(2,1)}) %reduce-scatter.8.cloned.1.call-update) | async-done | bytes 1179664 | tf_op jit(solution)/shard_map/reduce_scatter | solution.py:214
  623.5 1.6 convert_element_type.111
  625.7 0.9 multiply_reduce_fusion
  628.6 64.7 %all-reduce = (f32[]{:T(128)}, f32[]{:T(128)}) all-reduce(f32[]{:T(128)} %get-tuple-element.19, f32[]{:T(128)S(6)} %add.123), channel_id=1, replica_groups=mesh['dp'=16,'pipe'=8] {'dp','pipe'}, use_global_device_ids=true, to_apply=%region_8.9 | all-reduce | flops 2 | bytes 16 | tf_op jit(solution)/shard_map/psum | solution.py:187
  694.7 1.2 divide_bitcast_fusion
  695.9 1.8 copy.53
  697.7 1.3 copy.52
  (52 shorter events, 12.6 us)
Async XLA Ops:
  7.2 40.2 %all-gather.4.cloned.1.call-start = ((), (), s32[]{:S(2)}) async-start(), calls=%async_computation.4 | async-start | bytes 2228224 | tf_op jit(solution)/shard_map/all_gather | solution.py:142
  7.9 101.9 %all-gather.6.cloned.1.call-start = ((), (), s32[]{:S(2)}) async-start(), calls=%async_computation.5 | async-start | bytes 8912896 | tf_op jit(solution)/shard_map/all_gather | solution.py:137
  8.6 154.9 %all-gather.8.cloned.1.call-start = ((), (), s32[]{:S(2)}) async-start(), calls=%async_computation.6 | async-start | bytes 8912896 | tf_op jit(solution)/shard_map/all_gather | solution.py:174
  9.4 250.3 %reduce-scatter.4.cloned.1.call-start = ((), (), s32[]{:S(2)}) async-start(), calls=%async_computation.7 | async-start | bytes 4718592 | tf_op jit(solution)/shard_map/reduce_scatter | solution.py:176
  10.1 99.7 %copy-start.1 = (f32[8192]{0:T(1024)S(1)}, f32[8192]{0:T(1024)}, u32[]{:S(2)}) copy-start(f32[8192]{0:T(1024)} %param.12) | copy-start | bytes 98308
  118.1 45.4 %copy-start.3 = (f32[4,256,256]{1,2,0:T(8,128)}, f32[4,256,256]{1,2,0:T(8,128)S(1)}, u32[]{:S(2)}) copy-start(f32[4,256,256]{1,2,0:T(8,128)S(1)} %get-tuple-element.40) | copy-start | bytes 3145732
  163.5 7.9 %copy-start.2 = (bf16[32,8192]{1,0:T(8,128)(2,1)S(1)}, bf16[32,8192]{1,0:T(8,128)(2,1)}, u32[]{:S(2)}) copy-start(bf16[32,8192]{1,0:T(8,128)(2,1)} %param.9) | copy-start | bytes 1572868
  171.3 227.5 %reduce-scatter.6.cloned.1.call-start = ((), (), s32[]{:S(2)}) async-start(), calls=%async_computation.8 | async-start | bytes 589824 | tf_op jit(solution)/shard_map/reduce_scatter | solution.py:200
  171.4 18.4 %collective-permute-start = (bf16[32,8192]{1,0:T(8,128)(2,1)S(1)}, bf16[32,8192]{1,0:T(8,128)(2,1)S(1)}, u32[]{:S(2)}, u32[]{:S(2)}) collective-permute-start(bf16[32,8192]{1,0:T(8,128)(2,1)S(1)} %copy-done.2), channel_id=1, source_target_pairs={{0,1},{1,2},{2,3},{3,4},{4,5},{5,6},{6,7},{7,0},{8,9},{9,10},{10,1... | collective-permute-start | bytes 1572872 | tf_op jit(solution)/shard_map/ppermute | solution.py:29
  313.8 2.0 copy-start
  313.8 7.9 %copy-start.4 = (f32[4,256,256]{1,2,0:T(8,128)S(1)}, f32[4,256,256]{1,2,0:T(8,128)}, u32[]{:S(2)}) copy-start(f32[4,256,256]{1,2,0:T(8,128)} %copy-done.3) | copy-start | bytes 3145732
  328.4 295.0 %reduce-scatter.8.cloned.1.call-start = ((), (), s32[]{:S(2)}) async-start(), calls=%async_computation.9 | async-start | bytes 20054016 | tf_op jit(solution)/shard_map/reduce_scatter | solution.py:214
Sparse Core Ops, SparseCore 0:
  9.7 37.6 all-gather.3
  49.1 60.6 all-gather.5
  111.5 51.9 all-gather.7
  171.4 88.1 reduce-scatter.3
  328.6 70.1 reduce-scatter.5
  420.6 202.8 reduce-scatter.7
